TPU v7x, 32 devices: a whole 2x2x4 slice. The times are simulated.
32 devices in a mesh: grp: 4 (over y, core), dev: 8 (over z, x).
Axes of the slice: x: 2, y: 2, z: 4, core: 2. Of those that a mesh axis runs over, the one named last changes fastest.
Arguments:
- queries: bfloat16 [3072, 1024], P('dev'), may hold values from -16 to 16
- docs: bfloat16 [4096, 1024], P(('grp', 'dev')), may hold values from -16 to 16
- compat: int32 [24, 32], P('dev', 'grp'), may hold values from 0 to 1, as said below
- positives: int32 [3072], P('dev'), may hold values from 0 to 4095, as said below
Outputs:
- loss: float32 [3072], P('dev')
- query_grad: float32 [3072, 1024], P('dev')
- doc_grad: float32 [4096, 1024], P(('grp', 'dev'))
Inputs may be any that keep to these rules, and one draw needn't show every extreme that they name: compat[b, b % 32] is 1 for every query block b. positives[i] lies in a document block that is compatible with the block of query i.
All inputs are finite; a program needn't handle non-finite values.
Results may differ from a plain program's by a relative error of at most 0.0007.
Values may be sent and summed in bfloat16 or wider, within the bound.
A program may use at most 128 MiB of HBM per device.

v0:
```python
import jax
import jax.numpy as jnp
from jax import lax
from jax.sharding import PartitionSpec as P

BLOCK = 128


LOGIT_SCALE = 0.1
NEG_FLOOR = -1e30


def joined(value, axis, combine):
    everything = jax.tree.map(lambda part: lax.all_gather(part, axis), value)
    first = jax.tree.map(lambda part: part[0], everything)

    def hop(k, so_far):
        return combine(so_far, jax.tree.map(lambda part: part[k], everything))

    return lax.fori_loop(1, lax.axis_size(axis), hop, first)


def from_behind(value, axis, by):
    devices = lax.axis_size(axis)
    return lax.ppermute(value, axis, [(i, (i + by) % devices) for i in range(devices)])


def panel_scores(queries, panel):
    return LOGIT_SCALE * lax.dot_general(
        queries, panel, (((1,), (1,)), ((), ())), preferred_element_type=jnp.float32
    )


def panel_masks(compat, positives, column_start, doc_offset, block, panel_rows):
    blocks = lax.dynamic_slice_in_dim(compat, column_start, panel_rows // block, 1)
    live = jnp.repeat(jnp.repeat(blocks, block, axis=0), block, axis=1) > 0
    doc_ids = doc_offset + jnp.arange(panel_rows, dtype=jnp.int32)
    target = doc_ids[None, :] == positives[:, None]
    return (live, target)


def add_stats(stats, scores, live, target):
    row_max, total, chosen = stats
    local_max = jnp.max(jnp.where(live, scores, NEG_FLOOR), axis=1)
    new_max = jnp.maximum(row_max, local_max)
    terms = jnp.where(live, jnp.exp(scores - new_max[:, None]), 0.0)
    total = total * jnp.exp(row_max - new_max) + jnp.sum(terms, axis=1)
    chosen = chosen + jnp.sum(jnp.where(target, scores, 0.0), axis=1)
    return (new_max, total, chosen)


def merge_stats(first, second):
    top = jnp.maximum(first[0], second[0])
    total = first[1] * jnp.exp(first[0] - top) + second[1] * jnp.exp(second[0] - top)
    return (top, total, first[2] + second[2])


def finish_stats(stats):
    row_max, total, chosen = joined(stats, "grp", merge_stats)
    lse = row_max + jnp.log(total)
    return (lse, lse - chosen)


def coefficients(scores, live, target, lse):
    prob = jnp.where(live, jnp.exp(scores - lse[:, None]), 0.0)
    return (prob - target.astype(jnp.float32)).astype(jnp.bfloat16)


def local(queries, docs, compat, positives):
    width = lax.axis_size("dev")
    position = lax.axis_index("dev")
    group_index = lax.axis_index("grp")
    block = BLOCK
    panel_rows = docs.shape[0]
    query_rows = queries.shape[0]
    panel_blocks = panel_rows // block
    group_start = group_index * (width * panel_rows)
    empty_stats = (
        jnp.full((query_rows,), NEG_FLOOR, jnp.float32),
        jnp.zeros((query_rows,), jnp.float32),
        jnp.zeros((query_rows,), jnp.float32),
    )

    def masks_for(owner):
        return panel_masks(
            compat,
            positives,
            owner * panel_blocks,
            group_start + owner * panel_rows,
            block,
            panel_rows,
        )

    def visit(stats, panel, owner):
        live, target = masks_for(owner)
        scores = panel_scores(queries, panel)
        return (add_stats(stats, scores, live, target), scores)

    def gradient_step(carry, panel, scores, owner, lse):
        live, target = masks_for(owner)
        query_sum, doc_sum = carry
        coef = coefficients(scores, live, target, lse)
        query_sum = query_sum + LOGIT_SCALE * jnp.dot(
            coef, panel, preferred_element_type=jnp.float32
        )
        doc_sum = doc_sum + LOGIT_SCALE * lax.dot_general(
            coef, queries, (((0,), (0,)), ((), ())), preferred_element_type=jnp.float32
        )
        return (query_sum, doc_sum)

    stats, first_scores = visit(empty_stats, docs, position)
    store = jnp.zeros((width,) + docs.shape, docs.dtype).at[0].set(docs)
    score_store = jnp.zeros((width, query_rows, panel_rows), jnp.float32).at[0].set(first_scores)

    def first_turn(turn_index, carry):
        current, kept, kept_scores, partial_value = carry
        current = from_behind(current, "dev", 1)
        owner = (position - turn_index) % width
        kept = lax.dynamic_update_index_in_dim(kept, current, turn_index, 0)
        partial_value, scores = visit(partial_value, current, owner)
        kept_scores = lax.dynamic_update_index_in_dim(kept_scores, scores, turn_index, 0)
        return (current, kept, kept_scores, partial_value)

    current, store, score_store, stats = lax.fori_loop(
        1, width, first_turn, (docs, store, score_store, stats)
    )
    lse, loss = finish_stats(stats)
    start_carry = (
        jnp.zeros((query_rows, docs.shape[1]), jnp.float32),
        jnp.zeros((panel_rows, docs.shape[1]), jnp.float32),
    )
    start_carry = gradient_step(start_carry, docs, score_store[0], position, lse)

    def second_turn(turn_index, carry):
        query_sum, doc_sum = carry
        doc_sum = from_behind(doc_sum, "dev", 1)
        owner = (position - turn_index) % width
        panel = lax.dynamic_index_in_dim(store, turn_index, 0, keepdims=False)
        scores = lax.dynamic_index_in_dim(score_store, turn_index, 0, keepdims=False)
        return gradient_step((query_sum, doc_sum), panel, scores, owner, lse)

    query_part, doc_part = lax.fori_loop(1, width, second_turn, start_carry)
    doc_grad = from_behind(doc_part, "dev", 1)
    query_grad = lax.psum(query_part, "grp")
    return (loss, query_grad, doc_grad)


def solution(mesh):
    return jax.shard_map(
        local,
        mesh=mesh,
        in_specs=(P("dev", None), P(("grp", "dev"), None), P("dev", "grp"), P("dev")),
        out_specs=(P("dev"), P("dev", None), P(("grp", "dev"), None)),
        check_vma=False,
    )
```

profile of v0, /device:TPU:0, one launch (start us, length us, event | category | flops | bytes accessed | tf_op | source)
XLA Modules:
  0.0 280.5 jit_solution(13684167352823001613)
XLA Ops:
  7.2 0.8 copy.10
  8.0 0.9 fusion.28
  8.9 1.7 copy.28
  10.6 1.6 select_reduce_fusion.4
  12.4 1.2 scatter.9
  13.9 0.9 copy-done
  14.8 83.8 %while.67 = (s32[]{:T(128)}, bf16[128,1024]{1,0:T(8,128)(2,1)}, bf16[8,128,1024]{2,1,0:T(8,128)(2,1)S(1)}, f32[8,384,128]{1,2,0:T(8,128)}, f32[384]{0:T(512)S(1)...) while((s32[]{:T(128)}, bf16[128,1024]{1,0:T(8,128)(2,1)}, ...), condition=%wide.region_7.8_spmd, body=%wide.region_3.7_spmd.sunk | while | flops 101106560 | bytes 3962444 | solution.py:124
  14.8 2.9 %collective-permute-start = (bf16[128,1024]{1,0:T(8,128)(2,1)}, bf16[128,1024]{1,0:T(8,128)(2,1)S(1)}, u32[]{:S(2)}, u32[]{:S(2)}) collective-permute-start(bf16[128,1024]{1,0:T(8,128)(2,1)} %get-tuple-element.1277), channel_id=1, source_target_pairs={{0,1},{1,2},{2,3},{3,4},{4,5},{5,6},{6,7},{7,0},{8,9},{9,10},{10,1... | collective-permute-start | bytes 786440 | tf_op jit(solution)/shard_map/while/body/eval_jaxpr/ppermute | solution.py:25
  17.8 9.5 %collective-permute-done = bf16[128,1024]{1,0:T(8,128)(2,1)S(1)} collective-permute-done((bf16[128,1024]{1,0:T(8,128)(2,1)}, bf16[128,1024]{1,0:T(8,128)(2,1)S(1)}, u32[]{:S(2)}, u32[]{:S(2)}) %collective-permute-start) | collective-permute-done | bytes 262176 | tf_op jit(solution)/shard_map/while/body/eval_jaxpr/ppermute | solution.py:25
  27.3 1.1 bitcast_dynamic-update-slice_fusion.5
  28.5 0.7 copy.42
  29.5 10.2 %collective-permute-done = bf16[128,1024]{1,0:T(8,128)(2,1)S(1)} collective-permute-done((bf16[128,1024]{1,0:T(8,128)(2,1)}, bf16[128,1024]{1,0:T(8,128)(2,1)S(1)}, u32[]{:S(2)}, u32[]{:S(2)}) %collective-permute-start) | collective-permute-done | bytes 262176 | tf_op jit(solution)/shard_map/while/body/eval_jaxpr/ppermute | solution.py:25
  39.7 1.1 bitcast_dynamic-update-slice_fusion.5
  40.9 0.7 copy.42
  41.9 9.3 %collective-permute-done = bf16[128,1024]{1,0:T(8,128)(2,1)S(1)} collective-permute-done((bf16[128,1024]{1,0:T(8,128)(2,1)}, bf16[128,1024]{1,0:T(8,128)(2,1)S(1)}, u32[]{:S(2)}, u32[]{:S(2)}) %collective-permute-start) | collective-permute-done | bytes 262176 | tf_op jit(solution)/shard_map/while/body/eval_jaxpr/ppermute | solution.py:25
  51.2 1.1 bitcast_dynamic-update-slice_fusion.5
  52.5 0.7 copy.42
  53.4 9.1 %collective-permute-done = bf16[128,1024]{1,0:T(8,128)(2,1)S(1)} collective-permute-done((bf16[128,1024]{1,0:T(8,128)(2,1)}, bf16[128,1024]{1,0:T(8,128)(2,1)S(1)}, u32[]{:S(2)}, u32[]{:S(2)}) %collective-permute-start) | collective-permute-done | bytes 262176 | tf_op jit(solution)/shard_map/while/body/eval_jaxpr/ppermute | solution.py:25
  62.5 1.1 bitcast_dynamic-update-slice_fusion.5
  64.8 9.1 %collective-permute-done = bf16[128,1024]{1,0:T(8,128)(2,1)S(1)} collective-permute-done((bf16[128,1024]{1,0:T(8,128)(2,1)}, bf16[128,1024]{1,0:T(8,128)(2,1)S(1)}, u32[]{:S(2)}, u32[]{:S(2)}) %collective-permute-start) | collective-permute-done | bytes 262176 | tf_op jit(solution)/shard_map/while/body/eval_jaxpr/ppermute | solution.py:25
  73.9 1.1 bitcast_dynamic-update-slice_fusion.5
  76.1 9.1 %collective-permute-done = bf16[128,1024]{1,0:T(8,128)(2,1)S(1)} collective-permute-done((bf16[128,1024]{1,0:T(8,128)(2,1)}, bf16[128,1024]{1,0:T(8,128)(2,1)S(1)}, u32[]{:S(2)}, u32[]{:S(2)}) %collective-permute-start) | collective-permute-done | bytes 262176 | tf_op jit(solution)/shard_map/while/body/eval_jaxpr/ppermute | solution.py:25
  85.2 1.1 bitcast_dynamic-update-slice_fusion.5
  87.4 9.1 %collective-permute-done = bf16[128,1024]{1,0:T(8,128)(2,1)S(1)} collective-permute-done((bf16[128,1024]{1,0:T(8,128)(2,1)}, bf16[128,1024]{1,0:T(8,128)(2,1)S(1)}, u32[]{:S(2)}, u32[]{:S(2)}) %collective-permute-start) | collective-permute-done | bytes 262176 | tf_op jit(solution)/shard_map/while/body/eval_jaxpr/ppermute | solution.py:25
  96.5 1.1 bitcast_dynamic-update-slice_fusion.5
  98.5 5.2 %all-gather.5 = f32[4,1,384]{2,1,0:T(1,128)S(1)} all-gather(f32[1,1,384]{2,1,0:T(1,128)S(1)} %reshape.269), channel_id=4, replica_groups=mesh['grp'=4,'dev'=8] {'grp'}, dimensions={0}, use_global_device_ids=true | all-gather | bytes 7680 | tf_op jit(solution)/shard_map/all_gather | solution.py:14
  103.7 5.2 %all-gather.4 = f32[4,1,384]{2,1,0:T(1,128)S(1)} all-gather(f32[1,1,384]{2,1,0:T(1,128)S(1)} %reshape.267), channel_id=3, replica_groups=mesh['grp'=4,'dev'=8] {'grp'}, dimensions={0}, use_global_device_ids=true | all-gather | bytes 7680 | tf_op jit(solution)/shard_map/all_gather | solution.py:14
  108.9 5.2 %all-gather.3 = f32[4,1,384]{2,1,0:T(1,128)S(1)} all-gather(f32[1,1,384]{2,1,0:T(1,128)S(1)} %reshape.265), channel_id=2, replica_groups=mesh['grp'=4,'dev'=8] {'grp'}, dimensions={0}, use_global_device_ids=true | all-gather | bytes 7680 | tf_op jit(solution)/shard_map/all_gather | solution.py:14
  115.0 2.1 convolution_multiply_fusion.3
  117.1 1.4 convolution_multiply_fusion.2
  118.5 110.6 %while.69 = (s32[]{:T(128)}, f32[384,1024]{1,0:T(8,128)S(1)}, f32[128,1024]{1,0:T(8,128)}, s32[]{:T(128)}, s32[3,8]{0,1:T(8,128)S(1)}, /*index=5*/f32[8,384,128]...) while((s32[]{:T(128)}, f32[384,1024]{1,0:T(8,128)S(1)}, ...), condition=%wide.region_11.12_spmd, body=%wide.region_10.11_spmd.sunk | while | flops 202965152 | bytes 8528964 | solution.py:142
  118.6 0.9 constant_dynamic-slice_fusion.4
  119.8 1.5 multiply_add_fusion.9
  121.2 14.3 %collective-permute-done.1 = f32[128,1024]{1,0:T(8,128)S(1)} collective-permute-done((f32[128,1024]{1,0:T(8,128)}, f32[128,1024]{1,0:T(8,128)S(1)}, u32[]{:S(2)}, u32[]{:S(2)}) %collective-permute-start.1) | collective-permute-done | bytes 524320 | tf_op jit(solution)/shard_map/while/body/eval_jaxpr/ppermute | solution.py:25
  135.6 1.3 fusion.52
  136.9 0.9 constant_dynamic-slice_fusion.4
  138.1 1.5 multiply_add_fusion.9
  139.6 13.6 %collective-permute-done.1 = f32[128,1024]{1,0:T(8,128)S(1)} collective-permute-done((f32[128,1024]{1,0:T(8,128)}, f32[128,1024]{1,0:T(8,128)S(1)}, u32[]{:S(2)}, u32[]{:S(2)}) %collective-permute-start.1) | collective-permute-done | bytes 524320 | tf_op jit(solution)/shard_map/while/body/eval_jaxpr/ppermute | solution.py:25
  153.2 1.3 fusion.52
  154.5 0.9 constant_dynamic-slice_fusion.4
  155.7 1.5 multiply_add_fusion.9
  157.2 12.7 %collective-permute-done.1 = f32[128,1024]{1,0:T(8,128)S(1)} collective-permute-done((f32[128,1024]{1,0:T(8,128)}, f32[128,1024]{1,0:T(8,128)S(1)}, u32[]{:S(2)}, u32[]{:S(2)}) %collective-permute-start.1) | collective-permute-done | bytes 524320 | tf_op jit(solution)/shard_map/while/body/eval_jaxpr/ppermute | solution.py:25
  169.8 1.3 fusion.52
  171.2 0.9 constant_dynamic-slice_fusion.4
  172.3 1.5 multiply_add_fusion.9
  173.8 11.7 %collective-permute-done.1 = f32[128,1024]{1,0:T(8,128)S(1)} collective-permute-done((f32[128,1024]{1,0:T(8,128)}, f32[128,1024]{1,0:T(8,128)S(1)}, u32[]{:S(2)}, u32[]{:S(2)}) %collective-permute-start.1) | collective-permute-done | bytes 524320 | tf_op jit(solution)/shard_map/while/body/eval_jaxpr/ppermute | solution.py:25
  185.6 1.3 fusion.52
  186.9 0.9 constant_dynamic-slice_fusion.4
  188.1 1.5 multiply_add_fusion.9
  189.5 10.8 %collective-permute-done.1 = f32[128,1024]{1,0:T(8,128)S(1)} collective-permute-done((f32[128,1024]{1,0:T(8,128)}, f32[128,1024]{1,0:T(8,128)S(1)}, u32[]{:S(2)}, u32[]{:S(2)}) %collective-permute-start.1) | collective-permute-done | bytes 524320 | tf_op jit(solution)/shard_map/while/body/eval_jaxpr/ppermute | solution.py:25
  200.4 1.3 fusion.52
  201.7 0.9 constant_dynamic-slice_fusion.4
  202.9 1.5 multiply_add_fusion.9
  204.4 9.9 %collective-permute-done.1 = f32[128,1024]{1,0:T(8,128)S(1)} collective-permute-done((f32[128,1024]{1,0:T(8,128)}, f32[128,1024]{1,0:T(8,128)S(1)}, u32[]{:S(2)}, u32[]{:S(2)}) %collective-permute-start.1) | collective-permute-done | bytes 524320 | tf_op jit(solution)/shard_map/while/body/eval_jaxpr/ppermute | solution.py:25
  214.3 1.3 fusion.52
  215.6 0.9 constant_dynamic-slice_fusion.4
  216.8 1.5 multiply_add_fusion.9
  218.3 9.4 %collective-permute-done.1 = f32[128,1024]{1,0:T(8,128)S(1)} collective-permute-done((f32[128,1024]{1,0:T(8,128)}, f32[128,1024]{1,0:T(8,128)S(1)}, u32[]{:S(2)}, u32[]{:S(2)}) %collective-permute-start.1) | collective-permute-done | bytes 524320 | tf_op jit(solution)/shard_map/while/body/eval_jaxpr/ppermute | solution.py:25
  227.7 1.3 fusion.52
  229.0 1.1 copy-done.1
  230.4 11.9 %collective-permute-done.2 = f32[128,1024]{1,0:T(8,128)S(1)} collective-permute-done((f32[128,1024]{1,0:T(8,128)S(1)}, f32[128,1024]{1,0:T(8,128)S(1)}, u32[]{:S(2)}, u32[]{:S(2)}) %collective-permute-start.2) | collective-permute-done | bytes 524320 | tf_op jit(solution)/shard_map/ppermute | solution.py:25
  242.3 27.8 %all-reduce.4.cloned.1.call-done = f32[384,1024]{1,0:T(8,128)} async-done(((f32[384,1024]{1,0:T(8,128)}), f32[384,1024]{1,0:T(8,128)}) %all-reduce.4.cloned.1.call-update) | async-done | bytes 1572880 | tf_op jit(solution)/shard_map/psum | solution.py:144
  270.1 2.7 copy.71
  272.8 0.8 copy.72
  (157 shorter events, 8.7 us)
Async XLA Ops:
  7.2 5.1 %copy-start.4 = (s32[384]{0:T(512)S(1)}, s32[384]{0:T(512)}, u32[]{:S(2)}) copy-start(s32[384]{0:T(512)} %param.17) | copy-start | bytes 4612
  7.2 262.9 %all-reduce.4.cloned.1.call-start = ((), (), s32[]{:S(2)}) async-start(), calls=%async_computation | async-start | bytes 3145728 | tf_op jit(solution)/shard_map/psum | solution.py:144
  10.6 3.0 %copy-start.3 = (bf16[128,1024]{1,0:T(8,128)(2,1)S(1)}, bf16[128,1024]{1,0:T(8,128)(2,1)}, u32[]{:S(2)}) copy-start(bf16[128,1024]{1,0:T(8,128)(2,1)} %param.15) | copy-start | bytes 786436
  13.6 1.1 copy-start
  14.8 12.5 %collective-permute-start = (bf16[128,1024]{1,0:T(8,128)(2,1)}, bf16[128,1024]{1,0:T(8,128)(2,1)S(1)}, u32[]{:S(2)}, u32[]{:S(2)}) collective-permute-start(bf16[128,1024]{1,0:T(8,128)(2,1)} %get-tuple-element.1277), channel_id=1, source_target_pairs={{0,1},{1,2},{2,3},{3,4},{4,5},{5,6},{6,7},{7,0},{8,9},{9,10},{10,1... | collective-permute-start | bytes 786440 | tf_op jit(solution)/shard_map/while/body/eval_jaxpr/ppermute | solution.py:25
  29.2 10.4 %collective-permute-start = (bf16[128,1024]{1,0:T(8,128)(2,1)}, bf16[128,1024]{1,0:T(8,128)(2,1)S(1)}, u32[]{:S(2)}, u32[]{:S(2)}) collective-permute-start(bf16[128,1024]{1,0:T(8,128)(2,1)} %get-tuple-element.1277), channel_id=1, source_target_pairs={{0,1},{1,2},{2,3},{3,4},{4,5},{5,6},{6,7},{7,0},{8,9},{9,10},{10,1... | collective-permute-start | bytes 786440 | tf_op jit(solution)/shard_map/while/body/eval_jaxpr/ppermute | solution.py:25
  41.7 9.5 %collective-permute-start = (bf16[128,1024]{1,0:T(8,128)(2,1)}, bf16[128,1024]{1,0:T(8,128)(2,1)S(1)}, u32[]{:S(2)}, u32[]{:S(2)}) collective-permute-start(bf16[128,1024]{1,0:T(8,128)(2,1)} %get-tuple-element.1277), channel_id=1, source_target_pairs={{0,1},{1,2},{2,3},{3,4},{4,5},{5,6},{6,7},{7,0},{8,9},{9,10},{10,1... | collective-permute-start | bytes 786440 | tf_op jit(solution)/shard_map/while/body/eval_jaxpr/ppermute | solution.py:25
  53.2 9.3 %collective-permute-start = (bf16[128,1024]{1,0:T(8,128)(2,1)}, bf16[128,1024]{1,0:T(8,128)(2,1)S(1)}, u32[]{:S(2)}, u32[]{:S(2)}) collective-permute-start(bf16[128,1024]{1,0:T(8,128)(2,1)} %get-tuple-element.1277), channel_id=1, source_target_pairs={{0,1},{1,2},{2,3},{3,4},{4,5},{5,6},{6,7},{7,0},{8,9},{9,10},{10,1... | collective-permute-start | bytes 786440 | tf_op jit(solution)/shard_map/while/body/eval_jaxpr/ppermute | solution.py:25
  64.5 9.3 %collective-permute-start = (bf16[128,1024]{1,0:T(8,128)(2,1)}, bf16[128,1024]{1,0:T(8,128)(2,1)S(1)}, u32[]{:S(2)}, u32[]{:S(2)}) collective-permute-start(bf16[128,1024]{1,0:T(8,128)(2,1)} %get-tuple-element.1277), channel_id=1, source_target_pairs={{0,1},{1,2},{2,3},{3,4},{4,5},{5,6},{6,7},{7,0},{8,9},{9,10},{10,1... | collective-permute-start | bytes 786440 | tf_op jit(solution)/shard_map/while/body/eval_jaxpr/ppermute | solution.py:25
  75.9 9.3 %collective-permute-start = (bf16[128,1024]{1,0:T(8,128)(2,1)}, bf16[128,1024]{1,0:T(8,128)(2,1)S(1)}, u32[]{:S(2)}, u32[]{:S(2)}) collective-permute-start(bf16[128,1024]{1,0:T(8,128)(2,1)} %get-tuple-element.1277), channel_id=1, source_target_pairs={{0,1},{1,2},{2,3},{3,4},{4,5},{5,6},{6,7},{7,0},{8,9},{9,10},{10,1... | collective-permute-start | bytes 786440 | tf_op jit(solution)/shard_map/while/body/eval_jaxpr/ppermute | solution.py:25
  87.2 9.3 %collective-permute-start = (bf16[128,1024]{1,0:T(8,128)(2,1)}, bf16[128,1024]{1,0:T(8,128)(2,1)S(1)}, u32[]{:S(2)}, u32[]{:S(2)}) collective-permute-start(bf16[128,1024]{1,0:T(8,128)(2,1)} %get-tuple-element.1277), channel_id=1, source_target_pairs={{0,1},{1,2},{2,3},{3,4},{4,5},{5,6},{6,7},{7,0},{8,9},{9,10},{10,1... | collective-permute-start | bytes 786440 | tf_op jit(solution)/shard_map/while/body/eval_jaxpr/ppermute | solution.py:25
  98.5 16.5 %copy-start.2 = (bf16[8,128,1024]{2,1,0:T(8,128)(2,1)}, bf16[8,128,1024]{2,1,0:T(8,128)(2,1)S(1)}, u32[]{:S(2)}) copy-start(bf16[8,128,1024]{2,1,0:T(8,128)(2,1)S(1)} %get-tuple-element.1351) | copy-start | bytes 6291460
  118.5 17.1 %collective-permute-start.1 = (f32[128,1024]{1,0:T(8,128)}, f32[128,1024]{1,0:T(8,128)S(1)}, u32[]{:S(2)}, u32[]{:S(2)}) collective-permute-start(f32[128,1024]{1,0:T(8,128)} %get-tuple-element.1361), channel_id=1, source_target_pairs={{0,1},{1,2},{2,3},{3,4},{4,5},{5,6},{6,7},{7,0},{8,9},{9,10},{10,1... | collective-permute-start | bytes 1572872 | tf_op jit(solution)/shard_map/while/body/eval_jaxpr/ppermute | solution.py:25
  136.9 16.2 %collective-permute-start.1 = (f32[128,1024]{1,0:T(8,128)}, f32[128,1024]{1,0:T(8,128)S(1)}, u32[]{:S(2)}, u32[]{:S(2)}) collective-permute-start(f32[128,1024]{1,0:T(8,128)} %get-tuple-element.1361), channel_id=1, source_target_pairs={{0,1},{1,2},{2,3},{3,4},{4,5},{5,6},{6,7},{7,0},{8,9},{9,10},{10,1... | collective-permute-start | bytes 1572872 | tf_op jit(solution)/shard_map/while/body/eval_jaxpr/ppermute | solution.py:25
  154.5 15.3 %collective-permute-start.1 = (f32[128,1024]{1,0:T(8,128)}, f32[128,1024]{1,0:T(8,128)S(1)}, u32[]{:S(2)}, u32[]{:S(2)}) collective-permute-start(f32[128,1024]{1,0:T(8,128)} %get-tuple-element.1361), channel_id=1, source_target_pairs={{0,1},{1,2},{2,3},{3,4},{4,5},{5,6},{6,7},{7,0},{8,9},{9,10},{10,1... | collective-permute-start | bytes 1572872 | tf_op jit(solution)/shard_map/while/body/eval_jaxpr/ppermute | solution.py:25
  171.2 14.4 %collective-permute-start.1 = (f32[128,1024]{1,0:T(8,128)}, f32[128,1024]{1,0:T(8,128)S(1)}, u32[]{:S(2)}, u32[]{:S(2)}) collective-permute-start(f32[128,1024]{1,0:T(8,128)} %get-tuple-element.1361), channel_id=1, source_target_pairs={{0,1},{1,2},{2,3},{3,4},{4,5},{5,6},{6,7},{7,0},{8,9},{9,10},{10,1... | collective-permute-start | bytes 1572872 | tf_op jit(solution)/shard_map/while/body/eval_jaxpr/ppermute | solution.py:25
  186.9 13.5 %collective-permute-start.1 = (f32[128,1024]{1,0:T(8,128)}, f32[128,1024]{1,0:T(8,128)S(1)}, u32[]{:S(2)}, u32[]{:S(2)}) collective-permute-start(f32[128,1024]{1,0:T(8,128)} %get-tuple-element.1361), channel_id=1, source_target_pairs={{0,1},{1,2},{2,3},{3,4},{4,5},{5,6},{6,7},{7,0},{8,9},{9,10},{10,1... | collective-permute-start | bytes 1572872 | tf_op jit(solution)/shard_map/while/body/eval_jaxpr/ppermute | solution.py:25
  201.7 12.5 %collective-permute-start.1 = (f32[128,1024]{1,0:T(8,128)}, f32[128,1024]{1,0:T(8,128)S(1)}, u32[]{:S(2)}, u32[]{:S(2)}) collective-permute-start(f32[128,1024]{1,0:T(8,128)} %get-tuple-element.1361), channel_id=1, source_target_pairs={{0,1},{1,2},{2,3},{3,4},{4,5},{5,6},{6,7},{7,0},{8,9},{9,10},{10,1... | collective-permute-start | bytes 1572872 | tf_op jit(solution)/shard_map/while/body/eval_jaxpr/ppermute | solution.py:25
  215.6 12.1 %collective-permute-start.1 = (f32[128,1024]{1,0:T(8,128)}, f32[128,1024]{1,0:T(8,128)S(1)}, u32[]{:S(2)}, u32[]{:S(2)}) collective-permute-start(f32[128,1024]{1,0:T(8,128)} %get-tuple-element.1361), channel_id=1, source_target_pairs={{0,1},{1,2},{2,3},{3,4},{4,5},{5,6},{6,7},{7,0},{8,9},{9,10},{10,1... | collective-permute-start | bytes 1572872 | tf_op jit(solution)/shard_map/while/body/eval_jaxpr/ppermute | solution.py:25
  229.0 1.1 copy-start.1
  229.0 1.4 copy-start.5
  230.4 11.9 %collective-permute-start.2 = (f32[128,1024]{1,0:T(8,128)S(1)}, f32[128,1024]{1,0:T(8,128)S(1)}, u32[]{:S(2)}, u32[]{:S(2)}) collective-permute-start(f32[128,1024]{1,0:T(8,128)S(1)} %copy-done.5), channel_id=1, source_target_pairs={{0,1},{1,2},{2,3},{3,4},{4,5},{5,6},{6,7},{7,0},{8,9},{9,10},{10,1... | collective-permute-start | bytes 1572872 | tf_op jit(solution)/shard_map/ppermute | solution.py:25
Sparse Core Ops, SparseCore 0:
  230.3 39.7 all-reduce.3
where the time goes:
time: 281 us; the launch traced here: 280 us
  waiting for transfers between devices  188 us (67%)
  matrix products  32.2 us (11%)
  local copies, waits for them, and re-layouts  23.6 us (8%)
  blocking collectives  15.5 us (6%)
  between operations  14.1 us (5%)
  starting transfers between devices  3.4 us (1%)
  other arithmetic  3.12 us (1%)
    ppermute x15, waiting for transfers between devices, from_behind(): lax.ppermute(value, axis, [(i, (i + by) % devices) for i in range(devices)])  160 us
    psum x1, waiting for transfers between devices, local(): query_grad = lax.psum(query_part, 'grp')  27.8 us
    all_gather x3, blocking collectives, joined(): everything = jax.tree.map(lambda part: lax.all_gather(part, axis), value)  15.5 us
    dot_general x8, matrix products, gradient_step(): jnp.dot(coef, panel, preferred_element_type=jnp.float32)  11.7 us
    dot_general x8, matrix products, gradient_step(): lax.dot_general(coef, queries, (((0,), (0,)), ((), ())), preferred_elemen...  11.5 us
    dot_general x8, matrix products, panel_scores(): lax.dot_general(queries, panel, (((1,), (1,)), ((), ())), preferred_eleme...  9 us
    unnamed x21, local copies, waits for them, and re-layouts  7.47 us
    dynamic_slice x14, local copies, waits for them, and re-layouts, second_turn(): lax.dynamic_index_in_dim(score_store, turn_index, 0, keepdims=False)  7.44 us
  transfers between devices with their start and end apart: 16, of which 16 were waited for; matrix products, arithmetic and copies ran while one was open for 7% of the time, Pallas kernels for 0%

commit v1 on v0

v1 whole, which is shorter than its diff:
```python
import functools
import jax
import jax.numpy as jnp
from jax import lax
from jax.experimental import pallas as pl
from jax.experimental.pallas import tpu as pltpu
from jax.sharding import PartitionSpec as P

BLOCK = 128
LOGIT_SCALE = 0.1
NEG_FLOOR = -1e30
CHUNK = 256
MESH = pl.DeviceIdType.MESH


def nt_dot(a, b):
    return lax.dot_general(a, b, (((1,), (1,)), ((), ())), preferred_element_type=jnp.float32)


def kernel(A, B, C, q_ref, docs_ref, compat_ref, pos_ref,
           loss_ref, qg_ref, dg_ref,
           docs_all, q_all, scores, coef_t, coef, run, st_all, packs,
           q_part, k1_recv, y_all, dd, dd_recv,
           du_s, du_r, dn_s, dn_r, dx_s, dx_r,
           qu_s, qu_r, qd_s, qd_r, qy_s, qy_r, qk_s, qk_r,
           st_s, st_r, pk_s, pk_r,
           k1_s, k1_r, gy_s, gy_r, k2_s, k2_r, dd_s, dd_r):
    n = A * B
    G = 2 * C
    rows, width = q_ref.shape
    panel = docs_ref.shape[0]
    qblocks = rows // BLOCK
    per = panel // BLOCK
    quarter = rows // G
    chunks = width // CHUNK
    half = chunks // 2
    me = lax.axis_index("dev")
    g = lax.axis_index("grp")
    a, b = me // B, me % B
    c, k = g // 2, g % 2

    def push(src, dst, ss, rs, grp, dev):
        pltpu.make_async_remote_copy(
            src_ref=src, dst_ref=dst, send_sem=ss, recv_sem=rs,
            device_id=(grp, dev), device_id_type=MESH).start()

    def sent(like, ss, rs):
        pltpu.make_async_remote_copy(
            src_ref=like, dst_ref=like, send_sem=ss, recv_sem=rs,
            device_id=(g, me), device_id_type=MESH).wait_send()

    def arrive(dst, ss, rs):
        pltpu.make_async_remote_copy(
            src_ref=dst, dst_ref=dst, send_sem=ss, recv_sem=rs,
            device_id=(g, me), device_id_type=MESH).wait_recv()

    barrier = pltpu.get_barrier_semaphore()
    friends = [(g, lax.rem(a + r, A) * B + b) for r in range(1, A)]
    friends += [(g, a * B + lax.rem(b + r, B)) for r in range(1, B)]
    friends += [(lax.rem(g + r, G), me) for r in range(1, G)]
    for f in friends:
        pl.semaphore_signal(barrier, inc=1, device_id=f, device_id_type=MESH)
    pl.semaphore_wait(barrier, len(friends))

    up_ok, dn_ok = a + 1 < A, a >= 1

    def dslot(owner_row, col):
        return docs_all.at[pl.ds((owner_row * B + col) * panel, panel)]

    def docs_up(s, src):
        @pl.when(up_ok)
        def _():
            push(src, dslot(a - s, b), du_s.at[s], du_r.at[s], g, me + B)

    def docs_dn(s, src):
        @pl.when(dn_ok)
        def _():
            push(src, dslot(a + s, b), dn_s.at[s], dn_r.at[s], g, me - B)

    def docs_x(owner, src):
        for r in range(1, B):
            i = owner * (B - 1) + r - 1
            push(src, dslot(owner, b), dx_s.at[i], dx_r.at[i], g,
                 a * B + lax.rem(b + r, B))

    def docs_x_arrive(owner):
        for r in range(1, B):
            i = owner * (B - 1) + r - 1
            arrive(dslot(owner, lax.rem(b + B - r, B)), dx_s.at[i], dx_r.at[i])

    docs_up(0, docs_ref)
    docs_dn(0, docs_ref)
    docs_x(a, docs_ref)
    docs_all[pl.ds(me * panel, panel), :] = docs_ref[...]

    lane_block = lax.broadcasted_iota(jnp.int32, (1, rows), 1) // BLOCK
    own = packs.at[a]
    own[1:2, :] = pos_ref[...].astype(jnp.float32)
    for j in range(n * per):
        line = jnp.zeros((1, rows), jnp.int32)
        for i in range(qblocks):
            line = jnp.where(lane_block == i, compat_ref[i, j], line)
        own[2 + j:3 + j, :] = line.astype(jnp.float32)
    run[0:1, :] = jnp.full((1, rows), NEG_FLOOR, jnp.float32)
    run[1:2, :] = jnp.zeros((1, rows), jnp.float32)

    sub = lax.broadcasted_iota(jnp.int32, (BLOCK, rows), 0)

    def masks(pack, j):
        live = pack[pl.ds(2 + j, 1), :] > 0.0
        ids = (sub + (g * n * per + j) * BLOCK).astype(jnp.float32)
        return live, ids == pack[1:2, :]

    def score_row(owner):
        def one(t, carry):
            j = owner * B * per + t
            at = pl.ds(j * BLOCK, BLOCK)
            s = LOGIT_SCALE * nt_dot(docs_all[at, :], q_ref[...])
            scores[at, :] = s
            live, target = masks(own, j)
            top = jnp.max(jnp.where(live, s, NEG_FLOOR), axis=0, keepdims=True)
            run[0:1, :] = jnp.maximum(run[0:1, :], top)
            run[1:2, :] += jnp.sum(jnp.where(target, s, 0.0), axis=0, keepdims=True)
            return carry
        lax.fori_loop(0, B * per, one, 0)

    my_rows = pl.ds(g * quarter, quarter)

    def q_up(s, src):
        push(src, q_all.at[a - s, my_rows], qu_s.at[s], qu_r.at[s], g, me + B)

    def q_dn(s, src):
        push(src, q_all.at[a + s, my_rows], qd_s.at[s], qd_r.at[s], g, me - B)

    def q_start():
        @pl.when(up_ok)
        def _():
            q_up(0, q_ref.at[my_rows])

        @pl.when(dn_ok)
        def _():
            q_dn(0, q_ref.at[my_rows])

    def valid(s):
        return (a - 1 - s >= 0, a - 1 - s), (a + 1 + s < A, a + 1 + s)

    for s in range(A - 1):
        (uv, uo), (dv, do) = valid(s)

        @pl.when(uv)
        def _():
            arrive(dslot(uo, b), du_s.at[s], du_r.at[s])
            if s < A - 2:
                docs_up(s + 1, dslot(uo, b))
            docs_x(uo, dslot(uo, b))

        @pl.when(dv)
        def _():
            arrive(dslot(do, b), dn_s.at[s], dn_r.at[s])
            if s < A - 2:
                docs_dn(s + 1, dslot(do, b))
            docs_x(do, dslot(do, b))

        if s == max(A - 3, 0):
            q_start()
        if s == 0:
            docs_x_arrive(a)
            score_row(a)
        else:
            for ok, owner in valid(s - 1):
                @pl.when(ok)
                def _():
                    docs_x_arrive(owner)
                    score_row(owner)
    for ok, owner in valid(A - 2):
        @pl.when(ok)
        def _():
            docs_x_arrive(owner)
            score_row(owner)

    def q_relay(s):
        (uv, uo), (dv, do) = valid(s)

        def spread(owner):
            piece = q_all.at[owner, my_rows]
            for r in range(1, C):
                i = owner * (C - 1) + r - 1
                push(piece, piece, qy_s.at[i], qy_r.at[i],
                     lax.rem(c + r, C) * 2 + k, me)
            i = owner * C + c
            push(piece, piece, qk_s.at[i], qk_r.at[i], c * 2 + 1 - k, me)

        @pl.when(uv)
        def _():
            arrive(q_all.at[uo, my_rows], qu_s.at[s], qu_r.at[s])
            if s < A - 2:
                @pl.when(up_ok)
                def _():
                    q_up(s + 1, q_all.at[uo, my_rows])
            spread(uo)

        @pl.when(dv)
        def _():
            arrive(q_all.at[do, my_rows], qd_s.at[s], qd_r.at[s])
            if s < A - 2:
                @pl.when(dn_ok)
                def _():
                    q_dn(s + 1, q_all.at[do, my_rows])
            spread(do)

    def q_cross(s):
        for ok, owner in valid(s):
            @pl.when(ok)
            def _():
                for r in range(1, C):
                    i = owner * (C - 1) + r - 1
                    cc = lax.rem(c + C - r, C)
                    piece = q_all.at[owner, pl.ds((cc * 2 + k) * quarter, quarter)]
                    arrive(piece, qy_s.at[i], qy_r.at[i])
                    i = owner * C + cc
                    push(piece, piece, qk_s.at[i], qk_r.at[i], c * 2 + 1 - k, me)

    def q_arrive(owner):
        for cc in range(C):
            i = owner * C + cc
            piece = q_all.at[owner, pl.ds((cc * 2 + 1 - k) * quarter, quarter)]
            arrive(piece, qk_s.at[i], qk_r.at[i])

    top = run[0:1, :]

    def add_total(j, total):
        live, _ = masks(own, j)
        s = scores[pl.ds(j * BLOCK, BLOCK), :]
        terms = jnp.where(live, jnp.exp(s - top), 0.0)
        return total + jnp.sum(terms, axis=0, keepdims=True)

    total = lax.fori_loop(0, n * per, add_total, jnp.zeros((1, rows), jnp.float32))
    mine = st_all.at[g]
    mine[0:1, :] = top
    mine[1:2, :] = total
    mine[2:3, :] = run[1:2, :]
    for r in range(1, G):
        push(mine, mine, st_s.at[r - 1], st_r.at[r - 1], lax.rem(g + r, G), me)
    q_relay(0)
    for r in range(1, G):
        arrive(st_all.at[lax.rem(g + G - r, G)], st_s.at[r - 1], st_r.at[r - 1])
    top = st_all[0, 0:1, :]
    for i in range(1, G):
        top = jnp.maximum(top, st_all[i, 0:1, :])
    total = jnp.zeros((1, rows), jnp.float32)
    chosen = jnp.zeros((1, rows), jnp.float32)
    for i in range(G):
        total = total + st_all[i, 1:2, :] * jnp.exp(st_all[i, 0:1, :] - top)
        chosen = chosen + st_all[i, 2:3, :]
    lse = top + jnp.log(total)
    loss_ref[...] = lse - chosen
    own[0:1, :] = lse
    for r in range(1, A):
        push(own, own, pk_s.at[r - 1], pk_r.at[r - 1], g, lax.rem(a + r, A) * B + b)
    q_cross(0)

    def coef_block(j, carry):
        live, target = masks(own, j)
        at = pl.ds(j * BLOCK, BLOCK)
        prob = jnp.where(live, jnp.exp(scores[at, :] - lse), 0.0)
        coef_t[at, :] = (prob - target.astype(jnp.float32)).astype(jnp.bfloat16)
        return carry

    lax.fori_loop(0, n * per, coef_block, 0)
    coef[...] = coef_t[...].T
    if A > 2:
        q_relay(1)

    def grad_chunk(j):
        cols = pl.ds(pl.multiple_of(j * CHUNK, CHUNK), CHUNK)
        return LOGIT_SCALE * jnp.dot(coef[...], docs_all[:, cols],
                                     preferred_element_type=jnp.float32)

    other = c * 2 + 1 - k
    for t in range(half):
        q_part[t] = grad_chunk((1 - k) * half + t)
        push(q_part.at[t], k1_recv.at[t], k1_s.at[t], k1_r.at[t], other, me)
    if A > 2:
        q_cross(1)
    for t in range(half):
        part = grad_chunk(k * half + t)
        arrive(k1_recv.at[t], k1_s.at[t], k1_r.at[t])
        y_all[t, c] = part + k1_recv[t]
        for r in range(1, C):
            i = t * (C - 1) + r - 1
            push(y_all.at[t, c], y_all.at[t, c], gy_s.at[i], gy_r.at[i],
                 lax.rem(c + r, C) * 2 + k, me)
    for s in range(2, A - 1):
        q_relay(s)
        q_cross(s)

    def grad_docs(pack, queries, first):
        def one(t, carry):
            j = a * B * per + t
            at = pl.ds(j * BLOCK, BLOCK)
            s = LOGIT_SCALE * nt_dot(docs_all[at, :], queries[...])
            live, target = masks(pack, j)
            prob = jnp.where(live, jnp.exp(s - pack[0:1, :]), 0.0)
            cf = (prob - target.astype(jnp.float32)).astype(jnp.bfloat16)
            add = LOGIT_SCALE * jnp.dot(cf, queries[...], preferred_element_type=jnp.float32)
            to = pl.ds(t * BLOCK, BLOCK)
            dd[to, :] = add if first else dd[to, :] + add
            return carry
        lax.fori_loop(0, B * per, one, 0)

    grad_docs(own, q_ref, True)

    def remote_docs(s):
        (uv, uo), (dv, do) = valid(s)
        for ok, owner, i in ((uv, uo, s), (dv, do, A - 2 - s)):
            @pl.when(ok)
            def _():
                arrive(packs.at[owner], pk_s.at[i], pk_r.at[i])
                q_arrive(owner)
                grad_docs(packs.at[owner], q_all.at[owner], False)

    def finish_chunk(t):
        for r in range(1, C):
            i = t * (C - 1) + r - 1
            arrive(y_all.at[t, lax.rem(c + C - r, C)], gy_s.at[i], gy_r.at[i])
        value = y_all[t, 0]
        for i in range(1, C):
            value = value + y_all[t, i]
        cols = pl.ds(pl.multiple_of((k * half + t) * CHUNK, CHUNK), CHUNK)
        qg_ref[:, cols] = value
        push(qg_ref.at[:, cols], qg_ref.at[:, cols], k2_s.at[t], k2_r.at[t], other, me)

    for s in range(A - 1):
        remote_docs(s)
    for r in range(1, B):
        peer = lax.rem(b + r, B)
        push(dd.at[pl.ds(peer * panel, panel)], dd_recv.at[r - 1], dd_s.at[r - 1],
             dd_r.at[r - 1], g, a * B + peer)
    for t in range(half):
        finish_chunk(t)
    value = dd[pl.ds(b * panel, panel), :]
    for r in range(1, B):
        arrive(dd_recv.at[r - 1], dd_s.at[r - 1], dd_r.at[r - 1])
        value = value + dd_recv[r - 1]
    dg_ref[...] = value
    for t in range(half):
        cols = pl.ds(pl.multiple_of(((1 - k) * half + t) * CHUNK, CHUNK), CHUNK)
        arrive(qg_ref.at[:, cols], k2_s.at[t], k2_r.at[t])

    piece = q_ref.at[pl.ds(0, quarter)]
    for s in range(A - 1):
        @pl.when(jnp.logical_and(up_ok, a - s >= 0))
        def _():
            sent(docs_ref, du_s.at[s], du_r.at[s])
            sent(piece, qu_s.at[s], qu_r.at[s])

        @pl.when(jnp.logical_and(dn_ok, a + s < A))
        def _():
            sent(docs_ref, dn_s.at[s], dn_r.at[s])
            sent(piece, qd_s.at[s], qd_r.at[s])

        sent(own, pk_s.at[s], pk_r.at[s])
    for i in range(A * (B - 1)):
        sent(docs_ref, dx_s.at[i], dx_r.at[i])
    for owner in range(A):
        @pl.when(owner != a)
        def _():
            for i in range(owner * (C - 1), (owner + 1) * (C - 1)):
                sent(piece, qy_s.at[i], qy_r.at[i])
            for i in range(owner * C, (owner + 1) * C):
                sent(piece, qk_s.at[i], qk_r.at[i])
    for r in range(G - 1):
        sent(mine, st_s.at[r], st_r.at[r])
    for t in range(half):
        sent(q_part.at[t], k1_s.at[t], k1_r.at[t])
        cols = pl.ds(pl.multiple_of((k * half + t) * CHUNK, CHUNK), CHUNK)
        sent(qg_ref.at[:, cols], k2_s.at[t], k2_r.at[t])
        for i in range(t * (C - 1), (t + 1) * (C - 1)):
            sent(y_all.at[t, c], gy_s.at[i], gy_r.at[i])
    for r in range(B - 1):
        sent(dd_recv.at[r], dd_s.at[r], dd_r.at[r])


def local(grp, dev, queries, docs, compat, positives):
    A = 4 if dev % 4 == 0 else dev
    B = dev // A
    C = grp // 2
    rows, width = queries.shape
    panel = docs.shape[0]
    n = A * B
    half = width // CHUNK // 2
    pack_rows = -(-(2 + n * panel // BLOCK) // 8) * 8
    f32, bf16 = jnp.float32, jnp.bfloat16
    dma = pltpu.SemaphoreType.DMA
    sems = []
    for count in (A - 1, A - 1, A * (B - 1), A - 1, A - 1, A * (C - 1), A * C,
                  grp - 1, A - 1, half, half * (C - 1), half, B - 1):
        sems += [dma((max(count, 1),))] * 2
    vmem = pl.BlockSpec(memory_space=pltpu.VMEM)
    loss, query_grad, doc_grad = pl.pallas_call(
        functools.partial(kernel, A, B, C),
        out_shape=(
            jax.ShapeDtypeStruct((1, rows), f32),
            jax.ShapeDtypeStruct((rows, width), f32),
            jax.ShapeDtypeStruct((panel, width), f32),
        ),
        in_specs=[vmem, vmem, pl.BlockSpec(memory_space=pltpu.SMEM), vmem],
        out_specs=(vmem, vmem, vmem),
        scratch_shapes=[
            pltpu.VMEM((n * panel, width), bf16),
            pltpu.VMEM((A, rows, width), bf16),
            pltpu.VMEM((n * panel, rows), f32),
            pltpu.VMEM((n * panel, rows), bf16),
            pltpu.VMEM((rows, n * panel), bf16),
            pltpu.VMEM((8, rows), f32),
            pltpu.VMEM((grp, 8, rows), f32),
            pltpu.VMEM((A, pack_rows, rows), f32),
            pltpu.VMEM((half, rows, CHUNK), f32),
            pltpu.VMEM((half, rows, CHUNK), f32),
            pltpu.VMEM((half, C, rows, CHUNK), f32),
            pltpu.VMEM((B * panel, width), f32),
            pltpu.VMEM((max(B - 1, 1), panel, width), f32),
        ] + sems,
        compiler_params=pltpu.CompilerParams(
            collective_id=0, has_side_effects=True, vmem_limit_bytes=56 * 1024 * 1024),
    )(queries, docs, compat, positives.reshape(1, rows))
    return loss.reshape(rows), query_grad, doc_grad


def solution(mesh):
    return jax.shard_map(
        functools.partial(local, mesh.shape["grp"], mesh.shape["dev"]),
        mesh=mesh,
        in_specs=(P("dev", None), P(("grp", "dev"), None), P("dev", "grp"), P("dev")),
        out_specs=(P("dev"), P("dev", None), P(("grp", "dev"), None)),
        check_vma=False,
    )
```

time: 281 us -> 95.2 us (0.34)
  waiting for transfers between devices: 188 us -> 0 us
  Pallas kernels: 0 us -> 88.2 us
  matrix products: 32.2 us -> 0 us
  local copies, waits for them, and re-layouts: 23.6 us -> 4.83 us
  blocking collectives: 15.5 us -> 0 us
  between operations: 14.1 us -> 0.64 us
  starting transfers between devices: 3.4 us -> 0 us
    ppermute x15 -> x0, waiting for transfers between devices: 160 us -> none  [from_behind(): lax.ppermute(value, axis, [(i, (i + by) % devices) for i in range(devices)])]
    pallas_call x0 -> x1, Pallas kernels: none -> 88.2 us  [local(): pl.pallas_call(functools.partial(kernel, A, B, C), out_shape=(jax.ShapeDt...]
    dot_general x24 -> x0, matrix products: 32.2 us -> none  [the longest x8 11.7 us: gradient_step(): jnp.dot(coef, panel, preferred_element_type=jnp.float32)]
    psum x1 -> x0, waiting for transfers between devices: 27.8 us -> none  [local(): query_grad = lax.psum(query_part, 'grp')]
    all_gather x3 -> x0, blocking collectives: 15.5 us -> none  [joined(): everything = jax.tree.map(lambda part: lax.all_gather(part, axis), value)]
    dynamic_slice x20 -> x0, local copies, waits for them, and re-layouts: 7.59 us -> none  [the longest x14 7.44 us: second_turn(): lax.dynamic_index_in_dim(score_store, turn_index, 0, keepdims=False)]
    while x15 -> x0, local copies, waits for them, and re-layouts: 5.71 us -> none
    unnamed x21 -> x4, local copies, waits for them, and re-layouts: 7.47 us -> 3.58 us
  transfers between devices with their start and end apart: 16 -> 0, of which waited for: 16 -> 0; matrix products, arithmetic and copies ran while one was open for 7% -> 0% of each run, Pallas kernels for 0% -> 0%
where the time goes in v1:
time: 95.2 us; the launch traced here: 95 us
  Pallas kernels  88.2 us (93%)
  local copies, waits for them, and re-layouts  4.83 us (5%)
  other arithmetic  1.28 us (1%)
    pallas_call x1, Pallas kernels, local(): pl.pallas_call(functools.partial(kernel, A, B, C), out_shape=(jax.ShapeDt...  88.2 us
    unnamed x4, local copies, waits for them, and re-layouts  3.58 us

profile of v1, /device:TPU:0, one launch (start us, length us, event | category | flops | bytes accessed | tf_op | source)
XLA Modules:
  0.0 95.0 jit_solution(6631883583497457700)
XLA Ops:
  0.6 1.2 %reshape.12.pos_ref = s32[1,384]{1,0:T(1,128)} reshape(s32[384]{0:T(512)} %param.7) | data formatting | bytes 3072 | tf_op jit(solution)/shard_map/reshape | solution.py:426
  1.9 88.2 %shard_map.67 = (f32[1,384]{1,0:T(1,128)}, f32[384,1024]{1,0:T(8,128)}, f32[128,1024]{1,0:T(8,128)}) custom-call(bf16[384,1024]{1,0:T(8,128)(2,1)} %q_ref.1, bf16[128,1024]{1,0:T(8,128)(2,1)} %docs_ref.1, s32[3,8]{1,0:T(4,128)} %compat_ref.1, s32[1,384]{1,0:T(1,128)} %reshape.12.pos_ref), custom_call_target="tpu_custom_call" | custom-call | tf_op jit(solution)/shard_map/pallas_call | solution.py:400
  90.1 1.3 %reduce = f32[384]{0:T(512)} reduce(f32[1,384]{1,0:T(1,128)} %get-tuple-element.6, f32[]{:T(128)} %constant.1), dimensions={0}, to_apply=%get-tuple-element.6.reduce_sub_computation | reduce | bytes 3076 | tf_op jit(solution)/shard_map/pallas_call | solution.py:400
  91.4 0.0 copy-start
  91.4 2.8 %copy.9 = f32[384,1024]{1,0:T(8,128)} copy(f32[384,1024]{1,0:T(8,128)} %get-tuple-element.13) | data formatting | bytes 3145728
  94.2 0.0 copy-done
  94.2 0.8 copy.10
Async XLA Ops:
  91.4 2.8 %copy-start = (f32[128,1024]{1,0:T(8,128)S(1)}, f32[128,1024]{1,0:T(8,128)}, u32[]{:S(2)}) copy-start(f32[128,1024]{1,0:T(8,128)} %get-tuple-element.14) | copy-start | bytes 1572868

commit v2 on v1

--- a/solution.py
+++ b/solution.py
@@ -17,7 +17,7 @@
     return lax.dot_general(a, b, (((1,), (1,)), ((), ())), preferred_element_type=jnp.float32)
 
 
-def kernel(A, B, C, q_ref, docs_ref, compat_ref, pos_ref,
+def kernel(A, B, C, PD, PQ, q_ref, docs_ref, compat_ref, pos_ref,
            loss_ref, qg_ref, dg_ref,
            docs_all, q_all, scores, coef_t, coef, run, st_all, packs,
            q_part, k1_recv, y_all, dd, dd_recv,
@@ -32,6 +32,7 @@
     qblocks = rows // BLOCK
     per = panel // BLOCK
     quarter = rows // G
+    ph, qp = panel // PD, quarter // PQ
     chunks = width // CHUNK
     half = chunks // 2
     me = lax.axis_index("dev")
@@ -64,38 +65,43 @@
 
     up_ok, dn_ok = a + 1 < A, a >= 1
 
-    def dslot(owner_row, col):
-        return docs_all.at[pl.ds((owner_row * B + col) * panel, panel)]
-
-    def docs_up(s, src):
+    def dslot(owner_row, col, p):
+        return docs_all.at[pl.ds((owner_row * B + col) * panel + p * ph, ph)]
+
+    def docs_up(s, p, src):
         @pl.when(up_ok)
         def _():
-            push(src, dslot(a - s, b), du_s.at[s], du_r.at[s], g, me + B)
-
-    def docs_dn(s, src):
+            i = s * PD + p
+            push(src, dslot(a - s, b, p), du_s.at[i], du_r.at[i], g, me + B)
+
+    def docs_dn(s, p, src):
         @pl.when(dn_ok)
         def _():
-            push(src, dslot(a + s, b), dn_s.at[s], dn_r.at[s], g, me - B)
-
-    def docs_x(owner, src):
+            i = s * PD + p
+            push(src, dslot(a + s, b, p), dn_s.at[i], dn_r.at[i], g, me - B)
+
+    def docs_x(owner, p, src):
         for r in range(1, B):
-            i = owner * (B - 1) + r - 1
-            push(src, dslot(owner, b), dx_s.at[i], dx_r.at[i], g,
+            i = (owner * (B - 1) + r - 1) * PD + p
+            push(src, dslot(owner, b, p), dx_s.at[i], dx_r.at[i], g,
                  a * B + lax.rem(b + r, B))
 
     def docs_x_arrive(owner):
         for r in range(1, B):
-            i = owner * (B - 1) + r - 1
-            arrive(dslot(owner, lax.rem(b + B - r, B)), dx_s.at[i], dx_r.at[i])
-
-    docs_up(0, docs_ref)
-    docs_dn(0, docs_ref)
-    docs_x(a, docs_ref)
+            for p in range(PD):
+                i = (owner * (B - 1) + r - 1) * PD + p
+                arrive(dslot(owner, lax.rem(b + B - r, B), p), dx_s.at[i], dx_r.at[i])
+
+    for p in range(PD):
+        piece = docs_ref.at[pl.ds(p * ph, ph)]
+        docs_up(0, p, piece)
+        docs_dn(0, p, piece)
+        docs_x(a, p, piece)
     docs_all[pl.ds(me * panel, panel), :] = docs_ref[...]
 
     lane_block = lax.broadcasted_iota(jnp.int32, (1, rows), 1) // BLOCK
     own = packs.at[a]
-    own[1:2, :] = pos_ref[...].astype(jnp.float32)
+    own[1:2, :] = pos_ref[...].reshape(1, rows).astype(jnp.float32)
     for j in range(n * per):
         line = jnp.zeros((1, rows), jnp.int32)
         for i in range(qblocks):
@@ -124,22 +130,26 @@
             return carry
         lax.fori_loop(0, B * per, one, 0)
 
-    my_rows = pl.ds(g * quarter, quarter)
-
-    def q_up(s, src):
-        push(src, q_all.at[a - s, my_rows], qu_s.at[s], qu_r.at[s], g, me + B)
-
-    def q_dn(s, src):
-        push(src, q_all.at[a + s, my_rows], qd_s.at[s], qd_r.at[s], g, me - B)
+    def share(member, p):
+        return pl.ds(member * quarter + p * qp, qp)
+
+    def q_up(s, p, src):
+        i = s * PQ + p
+        push(src, q_all.at[a - s, share(g, p)], qu_s.at[i], qu_r.at[i], g, me + B)
+
+    def q_dn(s, p, src):
+        i = s * PQ + p
+        push(src, q_all.at[a + s, share(g, p)], qd_s.at[i], qd_r.at[i], g, me - B)
 
     def q_start():
-        @pl.when(up_ok)
-        def _():
-            q_up(0, q_ref.at[my_rows])
-
-        @pl.when(dn_ok)
-        def _():
-            q_dn(0, q_ref.at[my_rows])
+        for p in range(PQ):
+            @pl.when(up_ok)
+            def _():
+                q_up(0, p, q_ref.at[share(g, p)])
+
+            @pl.when(dn_ok)
+            def _():
+                q_dn(0, p, q_ref.at[share(g, p)])
 
     def valid(s):
         return (a - 1 - s >= 0, a - 1 - s), (a + 1 + s < A, a + 1 + s)
@@ -147,19 +157,22 @@
     for s in range(A - 1):
         (uv, uo), (dv, do) = valid(s)
 
-        @pl.when(uv)
-        def _():
-            arrive(dslot(uo, b), du_s.at[s], du_r.at[s])
-            if s < A - 2:
-                docs_up(s + 1, dslot(uo, b))
-            docs_x(uo, dslot(uo, b))
-
-        @pl.when(dv)
-        def _():
-            arrive(dslot(do, b), dn_s.at[s], dn_r.at[s])
-            if s < A - 2:
-                docs_dn(s + 1, dslot(do, b))
-            docs_x(do, dslot(do, b))
+        for p in range(PD):
+            @pl.when(uv)
+            def _():
+                i = s * PD + p
+                arrive(dslot(uo, b, p), du_s.at[i], du_r.at[i])
+                if s < A - 2:
+                    docs_up(s + 1, p, dslot(uo, b, p))
+                docs_x(uo, p, dslot(uo, b, p))
+
+            @pl.when(dv)
+            def _():
+                i = s * PD + p
+                arrive(dslot(do, b, p), dn_s.at[i], dn_r.at[i])
+                if s < A - 2:
+                    docs_dn(s + 1, p, dslot(do, b, p))
+                docs_x(do, p, dslot(do, b, p))
 
         if s == max(A - 3, 0):
             q_start()
@@ -172,59 +185,67 @@
                 def _():
                     docs_x_arrive(owner)
                     score_row(owner)
+    def q_relay(s):
+        (uv, uo), (dv, do) = valid(s)
+
+        def spread(owner, p):
+            piece = q_all.at[owner, share(g, p)]
+            for r in range(1, C):
+                i = (owner * (C - 1) + r - 1) * PQ + p
+                push(piece, piece, qy_s.at[i], qy_r.at[i],
+                     lax.rem(c + r, C) * 2 + k, me)
+            i = (owner * C + c) * PQ + p
+            push(piece, piece, qk_s.at[i], qk_r.at[i], c * 2 + 1 - k, me)
+
+        for p in range(PQ):
+            i = s * PQ + p
+
+            @pl.when(uv)
+            def _():
+                piece = q_all.at[uo, share(g, p)]
+                arrive(piece, qu_s.at[i], qu_r.at[i])
+                if s < A - 2:
+                    @pl.when(up_ok)
+                    def _():
+                        q_up(s + 1, p, piece)
+                spread(uo, p)
+
+            @pl.when(dv)
+            def _():
+                piece = q_all.at[do, share(g, p)]
+                arrive(piece, qd_s.at[i], qd_r.at[i])
+                if s < A - 2:
+                    @pl.when(dn_ok)
+                    def _():
+                        q_dn(s + 1, p, piece)
+                spread(do, p)
+
+    def q_cross(s):
+        for p in range(PQ):
+            for ok, owner in valid(s):
+                @pl.when(ok)
+                def _():
+                    for r in range(1, C):
+                        i = (owner * (C - 1) + r - 1) * PQ + p
+                        cc = lax.rem(c + C - r, C)
+                        piece = q_all.at[owner, share(cc * 2 + k, p)]
+                        arrive(piece, qy_s.at[i], qy_r.at[i])
+                        i = (owner * C + cc) * PQ + p
+                        push(piece, piece, qk_s.at[i], qk_r.at[i], c * 2 + 1 - k, me)
+
+    def q_arrive(owner):
+        for p in range(PQ):
+            for cc in range(C):
+                i = (owner * C + cc) * PQ + p
+                piece = q_all.at[owner, share(cc * 2 + 1 - k, p)]
+                arrive(piece, qk_s.at[i], qk_r.at[i])
+
+    q_relay(0)
     for ok, owner in valid(A - 2):
         @pl.when(ok)
         def _():
             docs_x_arrive(owner)
             score_row(owner)
-
-    def q_relay(s):
-        (uv, uo), (dv, do) = valid(s)
-
-        def spread(owner):
-            piece = q_all.at[owner, my_rows]
-            for r in range(1, C):
-                i = owner * (C - 1) + r - 1
-                push(piece, piece, qy_s.at[i], qy_r.at[i],
-                     lax.rem(c + r, C) * 2 + k, me)
-            i = owner * C + c
-            push(piece, piece, qk_s.at[i], qk_r.at[i], c * 2 + 1 - k, me)
-
-        @pl.when(uv)
-        def _():
-            arrive(q_all.at[uo, my_rows], qu_s.at[s], qu_r.at[s])
-            if s < A - 2:
-                @pl.when(up_ok)
-                def _():
-                    q_up(s + 1, q_all.at[uo, my_rows])
-            spread(uo)
-
-        @pl.when(dv)
-        def _():
-            arrive(q_all.at[do, my_rows], qd_s.at[s], qd_r.at[s])
-            if s < A - 2:
-                @pl.when(dn_ok)
-                def _():
-                    q_dn(s + 1, q_all.at[do, my_rows])
-            spread(do)
-
-    def q_cross(s):
-        for ok, owner in valid(s):
-            @pl.when(ok)
-            def _():
-                for r in range(1, C):
-                    i = owner * (C - 1) + r - 1
-                    cc = lax.rem(c + C - r, C)
-                    piece = q_all.at[owner, pl.ds((cc * 2 + k) * quarter, quarter)]
-                    arrive(piece, qy_s.at[i], qy_r.at[i])
-                    i = owner * C + cc
-                    push(piece, piece, qk_s.at[i], qk_r.at[i], c * 2 + 1 - k, me)
-
-    def q_arrive(owner):
-        for cc in range(C):
-            i = owner * C + cc
-            piece = q_all.at[owner, pl.ds((cc * 2 + 1 - k) * quarter, quarter)]
-            arrive(piece, qk_s.at[i], qk_r.at[i])
 
     top = run[0:1, :]
 
@@ -241,7 +262,8 @@
     mine[2:3, :] = run[1:2, :]
     for r in range(1, G):
         push(mine, mine, st_s.at[r - 1], st_r.at[r - 1], lax.rem(g + r, G), me)
-    q_relay(0)
+    if A > 2:
+        q_relay(1)
     for r in range(1, G):
         arrive(st_all.at[lax.rem(g + G - r, G)], st_s.at[r - 1], st_r.at[r - 1])
     top = st_all[0, 0:1, :]
@@ -253,7 +275,7 @@
         total = total + st_all[i, 1:2, :] * jnp.exp(st_all[i, 0:1, :] - top)
         chosen = chosen + st_all[i, 2:3, :]
     lse = top + jnp.log(total)
-    loss_ref[...] = lse - chosen
+    loss_ref[...] = (lse - chosen).reshape(rows)
     own[0:1, :] = lse
     for r in range(1, A):
         push(own, own, pk_s.at[r - 1], pk_r.at[r - 1], g, lax.rem(a + r, A) * B + b)
@@ -268,8 +290,6 @@
 
     lax.fori_loop(0, n * per, coef_block, 0)
     coef[...] = coef_t[...].T
-    if A > 2:
-        q_relay(1)
 
     def grad_chunk(j):
         cols = pl.ds(pl.multiple_of(j * CHUNK, CHUNK), CHUNK)
@@ -280,8 +300,6 @@
     for t in range(half):
         q_part[t] = grad_chunk((1 - k) * half + t)
         push(q_part.at[t], k1_recv.at[t], k1_s.at[t], k1_r.at[t], other, me)
-    if A > 2:
-        q_cross(1)
     for t in range(half):
         part = grad_chunk(k * half + t)
         arrive(k1_recv.at[t], k1_s.at[t], k1_r.at[t])
@@ -292,6 +310,7 @@
                  lax.rem(c + r, C) * 2 + k, me)
     for s in range(2, A - 1):
         q_relay(s)
+    for s in range(1, A - 1):
         q_cross(s)
 
     def grad_docs(pack, queries, first):
@@ -347,28 +366,33 @@
         cols = pl.ds(pl.multiple_of(((1 - k) * half + t) * CHUNK, CHUNK), CHUNK)
         arrive(qg_ref.at[:, cols], k2_s.at[t], k2_r.at[t])
 
-    piece = q_ref.at[pl.ds(0, quarter)]
+    qpiece = q_ref.at[pl.ds(0, qp)]
+    dpiece = docs_ref.at[pl.ds(0, ph)]
     for s in range(A - 1):
         @pl.when(jnp.logical_and(up_ok, a - s >= 0))
         def _():
-            sent(docs_ref, du_s.at[s], du_r.at[s])
-            sent(piece, qu_s.at[s], qu_r.at[s])
+            for i in range(s * PD, (s + 1) * PD):
+                sent(dpiece, du_s.at[i], du_r.at[i])
+            for i in range(s * PQ, (s + 1) * PQ):
+                sent(qpiece, qu_s.at[i], qu_r.at[i])
 
         @pl.when(jnp.logical_and(dn_ok, a + s < A))
         def _():
-            sent(docs_ref, dn_s.at[s], dn_r.at[s])
-            sent(piece, qd_s.at[s], qd_r.at[s])
+            for i in range(s * PD, (s + 1) * PD):
+                sent(dpiece, dn_s.at[i], dn_r.at[i])
+            for i in range(s * PQ, (s + 1) * PQ):
+                sent(qpiece, qd_s.at[i], qd_r.at[i])
 
         sent(own, pk_s.at[s], pk_r.at[s])
-    for i in range(A * (B - 1)):
-        sent(docs_ref, dx_s.at[i], dx_r.at[i])
+    for i in range(A * (B - 1) * PD):
+        sent(dpiece, dx_s.at[i], dx_r.at[i])
     for owner in range(A):
         @pl.when(owner != a)
         def _():
-            for i in range(owner * (C - 1), (owner + 1) * (C - 1)):
-                sent(piece, qy_s.at[i], qy_r.at[i])
-            for i in range(owner * C, (owner + 1) * C):
-                sent(piece, qk_s.at[i], qk_r.at[i])
+            for i in range(owner * (C - 1) * PQ, (owner + 1) * (C - 1) * PQ):
+                sent(qpiece, qy_s.at[i], qy_r.at[i])
+            for i in range(owner * C * PQ, (owner + 1) * C * PQ):
+                sent(qpiece, qk_s.at[i], qk_r.at[i])
     for r in range(G - 1):
         sent(mine, st_s.at[r], st_r.at[r])
     for t in range(half):
@@ -385,6 +409,8 @@
     A = 4 if dev % 4 == 0 else dev
     B = dev // A
     C = grp // 2
+    PD = 2
+    PQ = 2 if queries.shape[0] // grp % 32 == 0 else 1
     rows, width = queries.shape
     panel = docs.shape[0]
     n = A * B
@@ -393,14 +419,15 @@
     f32, bf16 = jnp.float32, jnp.bfloat16
     dma = pltpu.SemaphoreType.DMA
     sems = []
-    for count in (A - 1, A - 1, A * (B - 1), A - 1, A - 1, A * (C - 1), A * C,
+    for count in ((A - 1) * PD, (A - 1) * PD, A * (B - 1) * PD,
+                  (A - 1) * PQ, (A - 1) * PQ, A * (C - 1) * PQ, A * C * PQ,
                   grp - 1, A - 1, half, half * (C - 1), half, B - 1):
         sems += [dma((max(count, 1),))] * 2
     vmem = pl.BlockSpec(memory_space=pltpu.VMEM)
     loss, query_grad, doc_grad = pl.pallas_call(
-        functools.partial(kernel, A, B, C),
+        functools.partial(kernel, A, B, C, PD, PQ),
         out_shape=(
-            jax.ShapeDtypeStruct((1, rows), f32),
+            jax.ShapeDtypeStruct((rows,), f32),
             jax.ShapeDtypeStruct((rows, width), f32),
             jax.ShapeDtypeStruct((panel, width), f32),
         ),
@@ -423,8 +450,8 @@
         ] + sems,
         compiler_params=pltpu.CompilerParams(
             collective_id=0, has_side_effects=True, vmem_limit_bytes=56 * 1024 * 1024),
-    )(queries, docs, compat, positives.reshape(1, rows))
-    return loss.reshape(rows), query_grad, doc_grad
+    )(queries, docs, compat, positives)
+    return loss, query_grad, doc_grad
 
 
 def solution(mesh):

time: 95.2 us -> 91.6 us (0.962)
  Pallas kernels: 88.2 us -> 85.9 us
  other arithmetic: 1.28 us -> 0 us
    pallas_call x1, Pallas kernels: 88.2 us -> 85.9 us  [local(): pl.pallas_call(functools.partial(kernel, A, B, C, PD, PQ), out_shape=(jax...]
    pallas_call x1 -> x0, other arithmetic: 1.28 us -> none  [local(): pl.pallas_call(functools.partial(kernel, A, B, C), out_shape=(jax.ShapeDt...]
    unnamed x4 -> x5, local copies, waits for them, and re-layouts: 3.58 us -> 4.84 us
    reshape x1 -> x0, local copies, waits for them, and re-layouts: 1.25 us -> none  [local(): positives.reshape(1, rows)]
where the time goes in v2:
time: 91.6 us; the launch traced here: 91.4 us
  Pallas kernels  85.9 us (94%)
  local copies, waits for them, and re-layouts  4.84 us (5%)
    pallas_call x1, Pallas kernels, local(): pl.pallas_call(functools.partial(kernel, A, B, C, PD, PQ), out_shape=(jax...  85.9 us
    unnamed x5, local copies, waits for them, and re-layouts  4.84 us

profile of v2, /device:TPU:0, one launch (start us, length us, event | category | flops | bytes accessed | tf_op | source)
XLA Modules:
  0.0 91.4 jit_solution(10570482117126080629)
XLA Ops:
  0.6 85.9 %shard_map.67 = (f32[384]{0:T(512)}, f32[384,1024]{1,0:T(8,128)}, f32[128,1024]{1,0:T(8,128)}) custom-call(bf16[384,1024]{1,0:T(8,128)(2,1)} %q_ref.1, bf16[128,1024]{1,0:T(8,128)(2,1)} %docs_ref.1, s32[3,8]{1,0:T(4,128)} %compat_ref.1, s32[384]{0:T(512)} %pos_ref.1), custom_call_target="tpu_custom_call" | custom-call | tf_op jit(solution)/shard_map/pallas_call | solution.py:427
  86.6 1.3 %copy.10 = f32[384]{0:T(512)} copy(f32[384]{0:T(512)} %get-tuple-element.6) | data formatting | bytes 3072
  87.8 0.0 copy-start
  87.8 2.8 %copy.11 = f32[384,1024]{1,0:T(8,128)} copy(f32[384,1024]{1,0:T(8,128)} %get-tuple-element.7) | data formatting | bytes 3145728
  90.6 0.0 copy-done
  90.6 0.8 copy.12
Async XLA Ops:
  87.8 2.8 %copy-start = (f32[128,1024]{1,0:T(8,128)S(1)}, f32[128,1024]{1,0:T(8,128)}, u32[]{:S(2)}) copy-start(f32[128,1024]{1,0:T(8,128)} %get-tuple-element.8) | copy-start | bytes 1572868

commit v3 on v2

--- a/solution.py
+++ b/solution.py
@@ -110,17 +110,21 @@
     run[0:1, :] = jnp.full((1, rows), NEG_FLOOR, jnp.float32)
     run[1:2, :] = jnp.zeros((1, rows), jnp.float32)
 
-    sub = lax.broadcasted_iota(jnp.int32, (BLOCK, rows), 0)
+    PAIR = 2 if B * per % 2 == 0 else 1
+    span = PAIR * BLOCK
+    sub = lax.broadcasted_iota(jnp.int32, (span, rows), 0)
 
     def masks(pack, j):
-        live = pack[pl.ds(2 + j, 1), :] > 0.0
+        line = pack[pl.ds(2 + j, 1), :]
+        if PAIR == 2:
+            line = jnp.where(sub < BLOCK, line, pack[pl.ds(3 + j, 1), :])
         ids = (sub + (g * n * per + j) * BLOCK).astype(jnp.float32)
-        return live, ids == pack[1:2, :]
+        return line > 0.0, ids == pack[1:2, :]
 
     def score_row(owner):
         def one(t, carry):
-            j = owner * B * per + t
-            at = pl.ds(j * BLOCK, BLOCK)
+            j = owner * B * per + t * PAIR
+            at = pl.ds(j * BLOCK, span)
             s = LOGIT_SCALE * nt_dot(docs_all[at, :], q_ref[...])
             scores[at, :] = s
             live, target = masks(own, j)
@@ -128,7 +132,7 @@
             run[0:1, :] = jnp.maximum(run[0:1, :], top)
             run[1:2, :] += jnp.sum(jnp.where(target, s, 0.0), axis=0, keepdims=True)
             return carry
-        lax.fori_loop(0, B * per, one, 0)
+        lax.fori_loop(0, B * per // PAIR, one, 0)
 
     def share(member, p):
         return pl.ds(member * quarter + p * qp, qp)
@@ -154,37 +158,6 @@
     def valid(s):
         return (a - 1 - s >= 0, a - 1 - s), (a + 1 + s < A, a + 1 + s)
 
-    for s in range(A - 1):
-        (uv, uo), (dv, do) = valid(s)
-
-        for p in range(PD):
-            @pl.when(uv)
-            def _():
-                i = s * PD + p
-                arrive(dslot(uo, b, p), du_s.at[i], du_r.at[i])
-                if s < A - 2:
-                    docs_up(s + 1, p, dslot(uo, b, p))
-                docs_x(uo, p, dslot(uo, b, p))
-
-            @pl.when(dv)
-            def _():
-                i = s * PD + p
-                arrive(dslot(do, b, p), dn_s.at[i], dn_r.at[i])
-                if s < A - 2:
-                    docs_dn(s + 1, p, dslot(do, b, p))
-                docs_x(do, p, dslot(do, b, p))
-
-        if s == max(A - 3, 0):
-            q_start()
-        if s == 0:
-            docs_x_arrive(a)
-            score_row(a)
-        else:
-            for ok, owner in valid(s - 1):
-                @pl.when(ok)
-                def _():
-                    docs_x_arrive(owner)
-                    score_row(owner)
     def q_relay(s):
         (uv, uo), (dv, do) = valid(s)
 
@@ -240,7 +213,44 @@
                 piece = q_all.at[owner, share(cc * 2 + 1 - k, p)]
                 arrive(piece, qk_s.at[i], qk_r.at[i])
 
-    q_relay(0)
+    LAG = 2
+
+    def relay_at(point):
+        if 0 <= point - LAG < A - 1:
+            q_relay(point - LAG)
+
+    for s in range(A - 1):
+        (uv, uo), (dv, do) = valid(s)
+
+        for p in range(PD):
+            @pl.when(uv)
+            def _():
+                i = s * PD + p
+                arrive(dslot(uo, b, p), du_s.at[i], du_r.at[i])
+                if s < A - 2:
+                    docs_up(s + 1, p, dslot(uo, b, p))
+                docs_x(uo, p, dslot(uo, b, p))
+
+            @pl.when(dv)
+            def _():
+                i = s * PD + p
+                arrive(dslot(do, b, p), dn_s.at[i], dn_r.at[i])
+                if s < A - 2:
+                    docs_dn(s + 1, p, dslot(do, b, p))
+                docs_x(do, p, dslot(do, b, p))
+
+        if s == max(A - 3, 0):
+            q_start()
+        relay_at(s)
+        if s == 0:
+            docs_x_arrive(a)
+            score_row(a)
+        else:
+            for ok, owner in valid(s - 1):
+                @pl.when(ok)
+                def _():
+                    docs_x_arrive(owner)
+                    score_row(owner)
     for ok, owner in valid(A - 2):
         @pl.when(ok)
         def _():
@@ -249,21 +259,20 @@
 
     top = run[0:1, :]
 
-    def add_total(j, total):
-        live, _ = masks(own, j)
-        s = scores[pl.ds(j * BLOCK, BLOCK), :]
+    def add_total(t, total):
+        live, _ = masks(own, t * PAIR)
+        s = scores[pl.ds(t * span, span), :]
         terms = jnp.where(live, jnp.exp(s - top), 0.0)
         return total + jnp.sum(terms, axis=0, keepdims=True)
 
-    total = lax.fori_loop(0, n * per, add_total, jnp.zeros((1, rows), jnp.float32))
+    total = lax.fori_loop(0, n * per // PAIR, add_total, jnp.zeros((1, rows), jnp.float32))
     mine = st_all.at[g]
     mine[0:1, :] = top
     mine[1:2, :] = total
     mine[2:3, :] = run[1:2, :]
     for r in range(1, G):
         push(mine, mine, st_s.at[r - 1], st_r.at[r - 1], lax.rem(g + r, G), me)
-    if A > 2:
-        q_relay(1)
+    relay_at(A - 1)
     for r in range(1, G):
         arrive(st_all.at[lax.rem(g + G - r, G)], st_s.at[r - 1], st_r.at[r - 1])
     top = st_all[0, 0:1, :]
@@ -281,14 +290,14 @@
         push(own, own, pk_s.at[r - 1], pk_r.at[r - 1], g, lax.rem(a + r, A) * B + b)
     q_cross(0)
 
-    def coef_block(j, carry):
-        live, target = masks(own, j)
-        at = pl.ds(j * BLOCK, BLOCK)
+    def coef_block(t, carry):
+        live, target = masks(own, t * PAIR)
+        at = pl.ds(t * span, span)
         prob = jnp.where(live, jnp.exp(scores[at, :] - lse), 0.0)
         coef_t[at, :] = (prob - target.astype(jnp.float32)).astype(jnp.bfloat16)
         return carry
 
-    lax.fori_loop(0, n * per, coef_block, 0)
+    lax.fori_loop(0, n * per // PAIR, coef_block, 0)
     coef[...] = coef_t[...].T
 
     def grad_chunk(j):
@@ -300,6 +309,7 @@
     for t in range(half):
         q_part[t] = grad_chunk((1 - k) * half + t)
         push(q_part.at[t], k1_recv.at[t], k1_s.at[t], k1_r.at[t], other, me)
+    relay_at(A)
     for t in range(half):
         part = grad_chunk(k * half + t)
         arrive(k1_recv.at[t], k1_s.at[t], k1_r.at[t])
@@ -308,24 +318,22 @@
             i = t * (C - 1) + r - 1
             push(y_all.at[t, c], y_all.at[t, c], gy_s.at[i], gy_r.at[i],
                  lax.rem(c + r, C) * 2 + k, me)
-    for s in range(2, A - 1):
-        q_relay(s)
     for s in range(1, A - 1):
         q_cross(s)
 
     def grad_docs(pack, queries, first):
         def one(t, carry):
-            j = a * B * per + t
-            at = pl.ds(j * BLOCK, BLOCK)
+            j = a * B * per + t * PAIR
+            at = pl.ds(j * BLOCK, span)
             s = LOGIT_SCALE * nt_dot(docs_all[at, :], queries[...])
             live, target = masks(pack, j)
             prob = jnp.where(live, jnp.exp(s - pack[0:1, :]), 0.0)
             cf = (prob - target.astype(jnp.float32)).astype(jnp.bfloat16)
             add = LOGIT_SCALE * jnp.dot(cf, queries[...], preferred_element_type=jnp.float32)
-            to = pl.ds(t * BLOCK, BLOCK)
+            to = pl.ds(t * span, span)
             dd[to, :] = add if first else dd[to, :] + add
             return carry
-        lax.fori_loop(0, B * per, one, 0)
+        lax.fori_loop(0, B * per // PAIR, one, 0)
 
     grad_docs(own, q_ref, True)
 

time: 91.6 us -> 69.3 us (0.76)
  Pallas kernels: 85.9 us -> 63.7 us
    pallas_call x1, Pallas kernels: 85.9 us -> 63.7 us  [local(): pl.pallas_call(functools.partial(kernel, A, B, C, PD, PQ), out_shape=(jax...]
where the time goes in v3:
time: 69.3 us; the launch traced here: 69.2 us
  Pallas kernels  63.7 us (92%)
  local copies, waits for them, and re-layouts  4.84 us (7%)
    pallas_call x1, Pallas kernels, local(): pl.pallas_call(functools.partial(kernel, A, B, C, PD, PQ), out_shape=(jax...  63.7 us
    unnamed x5, local copies, waits for them, and re-layouts  4.84 us

profile of v3, /device:TPU:0, one launch (start us, length us, event | category | flops | bytes accessed | tf_op | source)
XLA Modules:
  0.0 69.2 jit_solution(2291999421499784337)
XLA Ops:
  0.6 63.7 %shard_map.67 = (f32[384]{0:T(512)}, f32[384,1024]{1,0:T(8,128)}, f32[128,1024]{1,0:T(8,128)}) custom-call(bf16[384,1024]{1,0:T(8,128)(2,1)} %q_ref.1, bf16[128,1024]{1,0:T(8,128)(2,1)} %docs_ref.1, s32[3,8]{1,0:T(4,128)} %compat_ref.1, s32[384]{0:T(512)} %pos_ref.1), custom_call_target="tpu_custom_call" | custom-call | tf_op jit(solution)/shard_map/pallas_call | solution.py:435
  64.3 1.3 %copy.10 = f32[384]{0:T(512)} copy(f32[384]{0:T(512)} %get-tuple-element.6) | data formatting | bytes 3072
  65.6 0.0 copy-start
  65.6 2.8 %copy.11 = f32[384,1024]{1,0:T(8,128)} copy(f32[384,1024]{1,0:T(8,128)} %get-tuple-element.7) | data formatting | bytes 3145728
  68.4 0.0 copy-done
  68.4 0.8 %copy.12 = f32[128,1024]{1,0:T(8,128)} copy(f32[128,1024]{1,0:T(8,128)S(1)} %copy-done) | data formatting | bytes 1048576
Async XLA Ops:
  65.6 2.8 %copy-start = (f32[128,1024]{1,0:T(8,128)S(1)}, f32[128,1024]{1,0:T(8,128)}, u32[]{:S(2)}) copy-start(f32[128,1024]{1,0:T(8,128)} %get-tuple-element.8) | copy-start | bytes 1572868
